TPU v7x, 32 devices: a whole 2x2x4 slice. The times are simulated.
32 devices in a mesh: row: 8 (over y, x, core), col: 4 (over z).
Axes of the slice: x: 2, y: 2, z: 4, core: 2. Of those that a mesh axis runs over, the one named last changes fastest.
Arguments:
- row_frames: float32 [3, 1024, 256], P(None, ('row', 'col')), may hold values from -40 to 40, as said below
- col_frames: float32 [3, 1024, 256], P(None, ('col', 'row')), may hold values from -40 to 40, as said below
- vectors: float32 [64, 1024], P(None, ('col', 'row')), may hold values from -6 to 6
Outputs:
- embedding_product: float32 [64, 1024], P(None, ('row', 'col'))
Inputs may be any that keep to these rules, and one draw needn't show every extreme that they name: `row_frames`: frames of one chain of 256 atoms, each rigidly rotated and moved and perturbed by its own amount. `col_frames`: frames of one chain of 256 atoms, each rigidly rotated and moved and perturbed by its own amount.
All inputs are finite; a program needn't handle non-finite values.
Results may differ from a plain program's by a relative error of at most 0.00017.
Values sent between devices are 32-bit elements; how exact they have to be, the bound alone decides.
No kernel may reach another device: no remote copies, remote signals or barrier semaphores. Data moves between devices by JAX's collectives and lax.ppermute only.
A program may use at most 64 MiB of HBM per device.

v0:
```python
import jax
import jax.numpy as jnp
from jax import lax
from jax.sharding import PartitionSpec as P

NEWTON = 8


band_width = 2.0


def centre(frames):
    return frames - jnp.mean(frames, axis=2, keepdims=True)


def kernel_tile(rows, cols):
    count_rows = rows.shape[1]
    count_cols = cols.shape[1]
    atoms = rows.shape[2]
    row_norms = jnp.sum(rows * rows, axis=(0, 2))
    col_norms = jnp.sum(cols * cols, axis=(0, 2))
    product = jnp.dot(
        cols.reshape(3 * count_cols, atoms),
        rows.reshape(3 * count_rows, atoms).T,
        precision=lax.Precision.HIGHEST,
        preferred_element_type=jnp.float32,
    )
    product = product.reshape(3, count_cols, 3, count_rows)
    moment = [[product[second, :, first, :] for second in range(3)] for first in range(3)]
    half_norm = 0.5 * (row_norms[None, :] + col_norms[:, None])
    coef_two = -2.0 * sum(
        (moment[first][second] * moment[first][second] for first in range(3) for second in range(3))
    )
    coef_one = 8.0 * (
        moment[0][0] * moment[1][2] * moment[2][1]
        + moment[1][1] * moment[2][0] * moment[0][2]
        + moment[2][2] * moment[0][1] * moment[1][0]
    ) - 8.0 * (
        moment[0][0] * moment[1][1] * moment[2][2]
        + moment[1][2] * moment[2][0] * moment[0][1]
        + moment[2][1] * moment[1][0] * moment[0][2]
    )
    trace_one = moment[0][0] + moment[1][1] + moment[2][2]
    key_matrix = [
        [
            trace_one,
            moment[1][2] - moment[2][1],
            moment[2][0] - moment[0][2],
            moment[0][1] - moment[1][0],
        ],
        [
            moment[1][2] - moment[2][1],
            moment[0][0] - moment[1][1] - moment[2][2],
            moment[0][1] + moment[1][0],
            moment[2][0] + moment[0][2],
        ],
        [
            moment[2][0] - moment[0][2],
            moment[0][1] + moment[1][0],
            -moment[0][0] + moment[1][1] - moment[2][2],
            moment[1][2] + moment[2][1],
        ],
        [
            moment[0][1] - moment[1][0],
            moment[2][0] + moment[0][2],
            moment[1][2] + moment[2][1],
            -moment[0][0] - moment[1][1] + moment[2][2],
        ],
    ]
    minor_top = [
        key_matrix[0][0] * key_matrix[1][1] - key_matrix[1][0] * key_matrix[0][1],
        key_matrix[0][0] * key_matrix[1][2] - key_matrix[1][0] * key_matrix[0][2],
        key_matrix[0][0] * key_matrix[1][3] - key_matrix[1][0] * key_matrix[0][3],
        key_matrix[0][1] * key_matrix[1][2] - key_matrix[1][1] * key_matrix[0][2],
        key_matrix[0][1] * key_matrix[1][3] - key_matrix[1][1] * key_matrix[0][3],
        key_matrix[0][2] * key_matrix[1][3] - key_matrix[1][2] * key_matrix[0][3],
    ]
    minor_low = [
        key_matrix[2][0] * key_matrix[3][1] - key_matrix[3][0] * key_matrix[2][1],
        key_matrix[2][0] * key_matrix[3][2] - key_matrix[3][0] * key_matrix[2][2],
        key_matrix[2][0] * key_matrix[3][3] - key_matrix[3][0] * key_matrix[2][3],
        key_matrix[2][1] * key_matrix[3][2] - key_matrix[3][1] * key_matrix[2][2],
        key_matrix[2][1] * key_matrix[3][3] - key_matrix[3][1] * key_matrix[2][3],
        key_matrix[2][2] * key_matrix[3][3] - key_matrix[3][2] * key_matrix[2][3],
    ]
    coef_zero = (
        minor_top[0] * minor_low[5]
        - minor_top[1] * minor_low[4]
        + minor_top[2] * minor_low[3]
        + minor_top[3] * minor_low[2]
        - minor_top[4] * minor_low[1]
        + minor_top[5] * minor_low[0]
    )
    eigen = half_norm
    for newton_step in range(NEWTON):
        eigen_sq = eigen * eigen
        value = (eigen_sq + coef_two) * eigen_sq + coef_one * eigen + coef_zero
        slope = 4.0 * eigen_sq * eigen + 2.0 * coef_two * eigen + coef_one
        eigen = eigen - value / slope
    squared = jnp.maximum(2.0 * (half_norm - eigen) / atoms, 0.0)
    return jnp.exp(-squared / band_width)


def per_device(row_frames, col_frames, vectors):
    rows_own = centre(row_frames)
    cols_own = centre(col_frames)
    panel_rows = lax.all_gather(rows_own, "col", axis=1, tiled=True)
    tile = kernel_tile(panel_rows, lax.all_gather(cols_own, "row", axis=1, tiled=True))
    weighted = jnp.dot(
        lax.all_gather(vectors, "row", axis=1, tiled=True),
        tile,
        precision=lax.Precision.HIGHEST,
        preferred_element_type=jnp.float32,
    )
    degree = jnp.sum(tile, axis=0, keepdims=True)
    summed, total = (
        lax.psum_scatter(weighted, "col", scatter_dimension=1, tiled=True),
        lax.psum_scatter(degree, "col", scatter_dimension=1, tiled=True),
    )
    return summed / total


def solution(mesh):
    return jax.shard_map(
        per_device,
        mesh=mesh,
        in_specs=(
            P(None, ("row", "col"), None),
            P(None, ("col", "row"), None),
            P(None, ("col", "row")),
        ),
        out_specs=P(None, ("row", "col")),
        check_vma=False,
    )
```

profile of v0, /device:TPU:0, one launch (start us, length us, event | category | flops | bytes accessed | tf_op | source)
XLA Modules:
  0.0 86.7 jit_solution(12211310897060958393)
XLA Ops:
  6.5 0.0 copy-start
  6.5 0.0 reduce-scatter.9.cloned.1.call-start
  6.5 1.0 %reduce_sum.47 = f32[3,32]{1,0:T(4,128)S(1)} reduce(f32[3,32,256]{2,1,0:T(8,128)} %param.4, f32[]{:T(128)} %constant.8.clone.1), dimensions={2}, to_apply=%region_2.0 | reduce | flops 24480 | bytes 98692 | tf_op jit(solution)/shard_map/reduce_sum | solution.py:13
  7.6 1.0 %broadcast_subtract_fusion = f32[3,32,256]{2,1,0:T(8,128)S(1)} fusion(f32[3,32,256]{2,1,0:T(8,128)} %param.4, f32[3,32]{1,0:T(4,128)S(1)} %broadcast_multiply_fusion), kind=kLoop, calls=%fused_computation.72 | loop fusion | flops 24576 | bytes 196992 | tf_op jit(solution)/shard_map/sub | solution.py:13
  8.5 11.9 %all_gather.10 = f32[3,256,256]{2,1,0:T(8,128)S(1)} all-gather(f32[3,32,256]{2,1,0:T(8,128)S(1)} %broadcast_subtract_fusion), channel_id=1, replica_groups=mesh['row'=8,'col'=4] {'row'}, dimensions={1}, use_global_device_ids=true | all-gather | bytes 884736 | tf_op jit(solution)/shard_map/all_gather | solution.py:108
  20.4 0.0 copy-done
  20.4 0.1 reduce_sum.45
  20.5 0.1 broadcast_subtract_fusion.1
  20.6 14.9 %all_gather.9 = f32[3,128,256]{2,1,0:T(8,128)S(1)} all-gather(f32[3,32,256]{2,1,0:T(8,128)S(1)} %broadcast_subtract_fusion.1), channel_id=1, replica_groups=mesh['row'=8,'col'=4] {'col'}, dimensions={1}, use_global_device_ids=true | all-gather | bytes 491520 | tf_op jit(solution)/shard_map/all_gather | solution.py:107
  35.5 0.1 multiply_reduce_fusion
  35.7 1.4 %fusion = f32[3,256,3,128]{3,1,2,0:T(8,128)S(1)} fusion(f32[3,256,256]{2,1,0:T(8,128)S(1)} %all_gather.10, f32[3,128,256]{2,1,0:T(8,128)S(1)} %all_gather.9), kind=kOutput, calls=%fused_computation.1 | convolution fusion | flops 905969664 | bytes 2359296 | tf_op jit(solution)/shard_map/dot_general | solution.py:22
  37.1 0.0 copy-start.1
  37.1 0.1 multiply_reduce_fusion.1
  37.2 1.0 %fusion.42 = (f32[128]{0:T(128)S(1)}, f32[256,128]{1,0:T(8,128)S(1)}) fusion(f32[3,256,3,128]{3,1,2,0:T(8,128)S(1)} %fusion, f32[256]{0:T(256)S(1)} %multiply_reduce_fusion, f32[128]{0:T(128)S(1)} %multiply_reduce_fusion.1), kind=kLoop, calls=%fused_computation.77 | loop fusion | flops 6586240 | bytes 1312768 | tf_op jit(solution)/shard_map/reduce_sum | solution.py:115
  38.2 0.7 copy.10
  38.9 0.0 reduce-scatter.9.cloned.1.call-update
  39.0 0.0 reduce-scatter.7.cloned.1.call-start
  39.0 0.0 copy-done.1
  39.0 9.2 %all_gather.11 = f32[64,256]{0,1:T(8,128)S(1)} all-gather(f32[64,32]{0,1:T(8,128)S(1)} %copy-done.1), channel_id=1, replica_groups=mesh['row'=8,'col'=4] {'row'}, dimensions={1}, use_global_device_ids=true | all-gather | bytes 73728 | tf_op jit(solution)/shard_map/all_gather | solution.py:110
  48.2 0.4 convolution_bitcast_fusion
  48.6 0.7 copy.8
  49.3 0.0 reduce-scatter.7.cloned.1.call-update
  49.3 9.6 %reduce-scatter.9.cloned.1.call-done = f32[32,1]{1,0:T(8,128)} async-done(((f32[128,1]{1,0:T(8,128)}), f32[32,1]{1,0:T(8,128)}) %reduce-scatter.9.cloned.1.call-update) | async-done | bytes 144
  59.0 0.8 copy.11
  59.7 18.7 %reduce-scatter.7.cloned.1.call-done = f32[32,64]{1,0:T(8,128)} async-done(((f32[128,64]{1,0:T(8,128)}), f32[32,64]{1,0:T(8,128)}) %reduce-scatter.7.cloned.1.call-update) | async-done | bytes 8208
  78.5 1.4 %bitcast_divide_fusion = f32[64,32]{0,1:T(8,128)} fusion(f32[32,64]{1,0:T(8,128)} %reduce-scatter.7.cloned.1.call-done, f32[32]{0:T(128)S(1)} %bitcast.86), kind=kLoop, calls=%fused_computation.74 | loop fusion | flops 2048 | bytes 16512 | tf_op jit(solution)/shard_map/div | solution.py:120
  (2 shorter events, 0.0 us)
Async XLA Ops:
  6.5 13.9 %copy-start = (f32[3,32,256]{2,1,0:T(8,128)S(1)}, f32[3,32,256]{2,1,0:T(8,128)}, u32[]{:S(2)}) copy-start(f32[3,32,256]{2,1,0:T(8,128)} %param.3) | copy-start | bytes 294916
  6.5 52.4 %reduce-scatter.9.cloned.1.call-start = ((), (), s32[]{:S(2)}) async-start(), calls=%async_computation.3 | async-start | bytes 81920
  37.1 2.0 %copy-start.1 = (f32[64,32]{0,1:T(8,128)S(1)}, f32[64,32]{0,1:T(8,128)}, u32[]{:S(2)}) copy-start(f32[64,32]{0,1:T(8,128)} %param.5) | copy-start | bytes 24580
  39.0 39.5 %reduce-scatter.7.cloned.1.call-start = ((), (), s32[]{:S(2)}) async-start(), calls=%async_computation.2 | async-start | bytes 81920
Sparse Core Ops, SparseCore 0:
  39.1 19.8 reduce-scatter.8
  61.3 17.1 reduce-scatter.6
where the time goes:
time: 87.1 us; the launch traced here: 86.7 us
  blocking collectives  36 us (41%)
  waiting for transfers between devices  28.4 us (33%)
  between operations  13.5 us (15%)
  other arithmetic  4.8 us (6%)
  local copies, waits for them, and re-layouts  2.27 us (3%)
  matrix products  1.76 us (2%)
    unnamed x4, waiting for transfers between devices  28.4 us
    all_gather x1, blocking collectives, per_device(): panel_rows = lax.all_gather(rows_own, 'col', axis=1, tiled=True)  14.9 us
    all_gather x1, blocking collectives, per_device(): lax.all_gather(cols_own, 'row', axis=1, tiled=True)  11.9 us
    all_gather x1, blocking collectives, per_device(): lax.all_gather(vectors, 'row', axis=1, tiled=True)  9.2 us
    unnamed x7, local copies, waits for them, and re-layouts  2.27 us
  transfers between devices with their start and end apart: 2, of which 2 were waited for; matrix products, arithmetic and copies ran while one was open for 2% of the time, Pallas kernels for 0%

commit v1 on v0

v1 whole, which is shorter than its diff:
```python
import functools

import jax
import jax.numpy as jnp
from jax import lax
from jax.experimental import pallas as pl
from jax.experimental.pallas import tpu as pltpu
from jax.sharding import PartitionSpec as P

NEWTON = 8
BAND = 2.0
LANES = 128
VM = pl.BlockSpec(memory_space=pltpu.VMEM)
NT = (((1,), (1,)), ((), ()))


def centre(frames):
    return frames - jnp.mean(frames, axis=-1, keepdims=True)


def split(x):
    high = x.astype(jnp.bfloat16)
    low = (x - high.astype(jnp.float32)).astype(jnp.bfloat16)
    return high, low


def pack_kernel(cols_ref, vec_ref, out_ref):
    comps, frames, atoms = cols_ref.shape
    nv = vec_ref.shape[1]
    for comp in range(comps):
        out_ref[comp * frames:(comp + 1) * frames, :] = centre(cols_ref[comp])
    groups = atoms // nv
    step = frames // groups
    out_ref[comps * frames:, :] = jnp.concatenate(
        [vec_ref[group * step:(group + 1) * step, :] for group in range(groups)], axis=1
    )


def eigen_tile(m, half_norm, atoms):
    s00, s01, s02, s10, s11, s12, s20, s21, s22 = m
    coef_two = -2.0 * (
        s00 * s00 + s01 * s01 + s02 * s02 + s10 * s10 + s11 * s11 + s12 * s12 + s20 * s20 + s21 * s21 + s22 * s22
    )
    coef_one = 8.0 * (s00 * s12 * s21 + s11 * s20 * s02 + s22 * s01 * s10) - 8.0 * (
        s00 * s11 * s22 + s12 * s20 * s01 + s21 * s10 * s02
    )
    k00 = s00 + s11 + s22
    k11 = s00 - s11 - s22
    k22 = s11 - s00 - s22
    k33 = s22 - s00 - s11
    k01 = s12 - s21
    k02 = s20 - s02
    k03 = s01 - s10
    k12 = s01 + s10
    k13 = s20 + s02
    k23 = s12 + s21
    top0 = k00 * k11 - k01 * k01
    top1 = k00 * k12 - k01 * k02
    top2 = k00 * k13 - k01 * k03
    top3 = k01 * k12 - k11 * k02
    top4 = k01 * k13 - k11 * k03
    top5 = k02 * k13 - k12 * k03
    low0 = k02 * k13 - k03 * k12
    low1 = k02 * k23 - k03 * k22
    low2 = k02 * k33 - k03 * k23
    low3 = k12 * k23 - k13 * k22
    low4 = k12 * k33 - k13 * k23
    low5 = k22 * k33 - k23 * k23
    coef_zero = top0 * low5 - top1 * low4 + top2 * low3 + top3 * low2 - top4 * low1 + top5 * low0
    eigen = half_norm
    twice = coef_two + coef_two
    for _ in range(NEWTON):
        eigen_sq = eigen * eigen
        value = (eigen_sq + coef_two) * eigen_sq + coef_one * eigen + coef_zero
        slope = (4.0 * eigen_sq + twice) * eigen + coef_one
        eigen = eigen - value / slope
    squared = jnp.maximum(2.0 * (half_norm - eigen) / atoms, 0.0)
    return jnp.exp(-squared / BAND)


def tile_kernel(n_rows, n_cols, frames, nv, *refs):
    row_refs = refs[:n_rows]
    col_refs = refs[n_rows:n_rows + n_cols]
    out_refs = refs[n_rows + n_cols:2 * n_rows + n_cols]
    moment, tile = refs[2 * n_rows + n_cols:]
    atoms = row_refs[0].shape[-1]
    count_cols = n_cols * frames
    per_group = max(1, min(n_rows, LANES // frames))
    groups = atoms // nv
    step = frames // groups

    cols = [
        jnp.concatenate([ref[comp * frames:(comp + 1) * frames, :] for ref in col_refs], axis=0) for comp in range(3)
    ]
    col_square = cols[0] * cols[0] + cols[1] * cols[1] + cols[2] * cols[2]
    col_norm = lax.dot_general(
        jnp.ones((8, atoms), jnp.float32), col_square, NT,
        precision=lax.Precision.HIGHEST, preferred_element_type=jnp.float32,
    )[0:1, :]
    col_high, col_low = split(jnp.concatenate(cols, axis=0))
    col_side = jnp.concatenate([col_high, col_high, col_low], axis=1)

    lane = lax.broadcasted_iota(jnp.int32, (step, LANES), 1)
    vec_parts = []
    for ref in col_refs:
        for group in range(groups):
            place = group * nv
            piece = ref[3 * frames:, place // LANES * LANES:place // LANES * LANES + LANES]
            if place % LANES:
                piece = pltpu.roll(piece, LANES - place % LANES, 1)
            vec_parts.append(jnp.where(lane < nv, piece, jnp.where(lane == nv, 1.0, 0.0)))
    vec_high, vec_low = split(jnp.concatenate(vec_parts, axis=0))
    vec_side = jnp.concatenate([vec_high, vec_high, vec_low], axis=0)

    for first in range(0, n_rows, per_group):
        slots = row_refs[first:first + per_group]
        count = len(slots) * frames
        rows = [centre(jnp.concatenate([ref[comp] for ref in slots], axis=0)) for comp in range(3)]
        row_norm = jnp.sum(rows[0] * rows[0] + rows[1] * rows[1] + rows[2] * rows[2], axis=1, keepdims=True)
        row_high, row_low = split(jnp.concatenate(rows, axis=0))
        moment[0:3 * count, :] = lax.dot_general(
            jnp.concatenate([row_high, row_low, row_high], axis=1), col_side, NT,
            preferred_element_type=jnp.float32,
        )
        for at in range(0, count, 8):
            m = [
                moment[a * count + at:a * count + at + 8, b * count_cols:(b + 1) * count_cols]
                for a in range(3) for b in range(3)
            ]
            half_norm = 0.5 * (row_norm[at:at + 8, :] + col_norm)
            tile[at:at + 8, :] = eigen_tile(m, half_norm, atoms)
        tile_high, tile_low = split(tile[0:count, :])
        product = jnp.dot(
            jnp.concatenate([tile_high, tile_low, tile_high], axis=1), vec_side, preferred_element_type=jnp.float32
        )
        for slot in range(len(slots)):
            out_refs[first + slot][...] = product[slot * frames:(slot + 1) * frames, :]


def finish_kernel(nv, *refs):
    total = refs[0][...]
    for ref in refs[1:-1]:
        total = total + ref[...]
    refs[-1][...] = total[:, 0:nv] / total[:, nv:nv + 1]


def per_device(n_row, n_col, row_frames, col_frames, vectors):
    comps, frames, atoms = row_frames.shape
    nv = vectors.shape[0]
    row_blocks = [row_frames] + [
        lax.ppermute(row_frames, "col", [(at, (at + shift) % n_col) for at in range(n_col)])
        for shift in range(1, n_col)
    ]
    packed = pl.pallas_call(
        pack_kernel,
        out_shape=jax.ShapeDtypeStruct((comps * frames + frames * nv // atoms, atoms), jnp.float32),
        in_specs=[VM, VM],
        out_specs=VM,
        name="centre_pack",
    )(col_frames, vectors.T)
    col_blocks = [packed] + [
        lax.ppermute(packed, "row", [(at, (at + shift) % n_row) for at in range(n_row)])
        for shift in range(1, n_row)
    ]
    group = max(1, min(n_col, LANES // frames)) * frames
    partial = pl.pallas_call(
        functools.partial(tile_kernel, n_col, n_row, frames, nv),
        out_shape=[jax.ShapeDtypeStruct((frames, LANES), jnp.float32)] * n_col,
        in_specs=[VM] * (n_col + n_row),
        out_specs=[VM] * n_col,
        scratch_shapes=[
            pltpu.VMEM((3 * group, 3 * n_row * frames), jnp.float32),
            pltpu.VMEM((group, n_row * frames), jnp.float32),
        ],
        compiler_params=pltpu.CompilerParams(vmem_limit_bytes=40 * 1024 * 1024),
        name="kernel_tile",
    )(*row_blocks, *col_blocks)
    shares = [partial[0]] + [
        lax.ppermute(partial[shift], "col", [(at, (at - shift) % n_col) for at in range(n_col)])
        for shift in range(1, n_col)
    ]
    result = pl.pallas_call(
        functools.partial(finish_kernel, nv),
        out_shape=jax.ShapeDtypeStruct((frames, nv), jnp.float32),
        in_specs=[VM] * n_col,
        out_specs=VM,
        name="sum_divide",
    )(*shares)
    return result.T


def solution(mesh):
    return jax.shard_map(
        functools.partial(per_device, mesh.shape["row"], mesh.shape["col"]),
        mesh=mesh,
        in_specs=(
            P(None, ("row", "col"), None),
            P(None, ("col", "row"), None),
            P(None, ("col", "row")),
        ),
        out_specs=P(None, ("row", "col")),
        check_vma=False,
    )
```

time: 87.1 us -> 42.7 us (0.49)
  blocking collectives: 36 us -> 0 us
  starting transfers between devices: 0.04 us -> 18.8 us
  between operations: 13.5 us -> 0.04 us
  waiting for transfers between devices: 28.4 us -> 16.2 us
  Pallas kernels: 0 us -> 5.32 us
  other arithmetic: 4.8 us -> 0 us
  matrix products: 1.76 us -> 0 us
    all_gather x3 -> x0, blocking collectives: 36 us -> none  [the longest x1 14.9 us: per_device(): panel_rows = lax.all_gather(rows_own, 'col', axis=1, tiled=True)]
    unnamed x4 -> x0, waiting for transfers between devices: 28.4 us -> none
    ppermute x0 -> x13, starting transfers between devices: none -> 18.8 us  [the longest x7 7.02 us: per_device(): lax.ppermute(packed, 'row', [(at, (at + shift) % n_row) for at in range(n...]
    ppermute x0 -> x13, waiting for transfers between devices: none -> 16.2 us  [the longest x7 7.97 us: per_device(): lax.ppermute(packed, 'row', [(at, (at + shift) % n_row) for at in range(n...]
    pallas_call x0 -> x3, Pallas kernels: none -> 5.32 us  [the longest x1 2.19 us: per_device(): pl.pallas_call(functools.partial(tile_kernel, n_col, n_row, frames, nv),...]
    reduce_sum x5 -> x0, other arithmetic: 2.35 us -> none  [the longest x2 1.11 us: centre(): return frames - jnp.mean(frames, axis=2, keepdims=True)]
    dot_general x2 -> x0, matrix products: 1.76 us -> none  [the longest x1 1.4 us: kernel_tile(): jnp.dot(cols.reshape(3 * count_cols, atoms), rows.reshape(3 * count_rows,...]
    div x3 -> x0, other arithmetic: 1.41 us -> none  [the longest x1 1.4 us: per_device(): return summed / total]
  transfers between devices with their start and end apart: 2 -> 13, of which waited for: 2 -> 7; matrix products, arithmetic and copies ran while one was open for 2% -> 0% of each run, Pallas kernels for 0% -> 0%
where the time goes in v1:
time: 42.7 us; the launch traced here: 42.4 us
  starting transfers between devices  18.8 us (44%)
  waiting for transfers between devices  16.2 us (38%)
  Pallas kernels  5.32 us (12%)
  local copies, waits for them, and re-layouts  2.09 us (5%)
    ppermute x7, waiting for transfers between devices, per_device(): lax.ppermute(packed, 'row', [(at, (at + shift) % n_row) for at in range(n...  7.97 us
    ppermute x7, starting transfers between devices, per_device(): lax.ppermute(packed, 'row', [(at, (at + shift) % n_row) for at in range(n...  7.02 us
    ppermute x3, starting transfers between devices, per_device(): lax.ppermute(row_frames, 'col', [(at, (at + shift) % n_col) for at in ran...  6.41 us
    ppermute x3, starting transfers between devices, per_device(): lax.ppermute(partial[shift], 'col', [(at, (at - shift) % n_col) for at in...  5.38 us
    ppermute x3, waiting for transfers between devices, per_device(): lax.ppermute(row_frames, 'col', [(at, (at + shift) % n_col) for at in ran...  4.71 us
    ppermute x3, waiting for transfers between devices, per_device(): lax.ppermute(partial[shift], 'col', [(at, (at - shift) % n_col) for at in...  3.51 us
    pallas_call x1, Pallas kernels, per_device(): pl.pallas_call(functools.partial(tile_kernel, n_col, n_row, frames, nv),...  2.19 us
    unnamed x12, local copies, waits for them, and re-layouts  2.09 us
  transfers between devices with their start and end apart: 13, of which 7 were waited for; matrix products, arithmetic and copies ran while one was open for 0% of the time, Pallas kernels for 0%

profile of v1, /device:TPU:0, one launch (start us, length us, event | category | flops | bytes accessed | tf_op | source)
XLA Modules:
  0.0 42.4 jit_solution(8333583974144398291)
XLA Ops:
  0.0 1.7 %centre_pack.1.refs_4_ = f32[104,256]{1,0:T(8,128)} custom-call(f32[3,32,256]{2,1,0:T(8,128)} %cols_ref.1, f32[32,64]{1,0:T(8,128)} %bitcast.2), custom_call_target="tpu_custom_call" | custom-call | tf_op jit(solution)/shard_map/centre_pack/pallas_call | solution.py:154
  1.7 3.3 %collective-permute-start.9 = (f32[104,256]{1,0:T(8,128)}, f32[104,256]{1,0:T(8,128)S(1)}, u32[]{:S(2)}, u32[]{:S(2)}) collective-permute-start(f32[104,256]{1,0:T(8,128)} %centre_pack.1.refs_4_), channel_id=1, source_target_pairs={{0,28},{4,0},{8,4},{12,8},{16,12},{20,16},{24,20},{28,24},{1,29},{... | collective-permute-start | bytes 319496 | tf_op jit(solution)/shard_map/ppermute | solution.py:162
  5.0 0.6 %collective-permute-start.8 = (f32[104,256]{1,0:T(8,128)}, f32[104,256]{1,0:T(8,128)S(1)}, u32[]{:S(2)}, u32[]{:S(2)}) collective-permute-start(f32[104,256]{1,0:T(8,128)} %centre_pack.1.refs_4_), channel_id=1, source_target_pairs={{0,24},{4,28},{8,0},{12,4},{16,8},{20,12},{24,16},{28,20},{1,25},{... | collective-permute-start | bytes 319496 | tf_op jit(solution)/shard_map/ppermute | solution.py:162
  5.6 2.6 %collective-permute-start.1 = (f32[3,32,256]{2,1,0:T(8,128)S(1)}, f32[3,32,256]{2,1,0:T(8,128)S(1)}, u32[]{:S(2)}, u32[]{:S(2)}) collective-permute-start(f32[3,32,256]{2,1,0:T(8,128)S(1)} %copy-done.1), channel_id=1, source_target_pairs={{0,2},{1,3},{2,0},{3,1},{4,6},{5,7},{6,4},{7,5},{8,10},{9,11},{10,... | collective-permute-start | bytes 294920 | tf_op jit(solution)/shard_map/ppermute | solution.py:151
  8.2 1.6 %collective-permute-start = (f32[3,32,256]{2,1,0:T(8,128)S(1)}, f32[3,32,256]{2,1,0:T(8,128)S(1)}, u32[]{:S(2)}, u32[]{:S(2)}) collective-permute-start(f32[3,32,256]{2,1,0:T(8,128)S(1)} %copy-done.1), channel_id=1, source_target_pairs={{0,1},{1,2},{2,3},{3,0},{4,5},{5,6},{6,7},{7,4},{8,9},{9,10},{10,1... | collective-permute-start | bytes 294920 | tf_op jit(solution)/shard_map/ppermute | solution.py:151
  9.7 2.2 %collective-permute-start.2 = (f32[3,32,256]{2,1,0:T(8,128)S(1)}, f32[3,32,256]{2,1,0:T(8,128)S(1)}, u32[]{:S(2)}, u32[]{:S(2)}) collective-permute-start(f32[3,32,256]{2,1,0:T(8,128)S(1)} %copy-done.1), channel_id=1, source_target_pairs={{0,3},{1,0},{2,1},{3,2},{4,7},{5,4},{6,5},{7,6},{8,11},{9,8},{10,9... | collective-permute-start | bytes 294920 | tf_op jit(solution)/shard_map/ppermute | solution.py:151
  12.0 4.4 %collective-permute-done.1.refs_2_ = f32[3,32,256]{2,1,0:T(8,128)S(1)} collective-permute-done((f32[3,32,256]{2,1,0:T(8,128)S(1)}, f32[3,32,256]{2,1,0:T(8,128)S(1)}, u32[]{:S(2)}, u32[]{:S(2)}) %collective-permute-start.1) | collective-permute-done | bytes 98336 | tf_op jit(solution)/shard_map/ppermute | solution.py:151
  16.4 0.0 collective-permute-start.7
  16.4 0.0 collective-permute-done.refs_1_
  16.4 0.5 %collective-permute-start.6 = (f32[104,256]{1,0:T(8,128)}, f32[104,256]{1,0:T(8,128)S(1)}, u32[]{:S(2)}, u32[]{:S(2)}) collective-permute-start(f32[104,256]{1,0:T(8,128)} %centre_pack.1.refs_4_), channel_id=1, source_target_pairs={{0,16},{4,20},{8,24},{12,28},{16,0},{20,4},{24,8},{28,12},{1,17},{... | collective-permute-start | bytes 319496 | tf_op jit(solution)/shard_map/ppermute | solution.py:162
  16.9 0.3 collective-permute-done.2.refs_3_
  17.2 1.1 %collective-permute-start.5 = (f32[104,256]{1,0:T(8,128)}, f32[104,256]{1,0:T(8,128)S(1)}, u32[]{:S(2)}, u32[]{:S(2)}) collective-permute-start(f32[104,256]{1,0:T(8,128)} %centre_pack.1.refs_4_), channel_id=1, source_target_pairs={{0,12},{4,16},{8,20},{12,24},{16,28},{20,0},{24,4},{28,8},{1,13},{... | collective-permute-start | bytes 319496 | tf_op jit(solution)/shard_map/ppermute | solution.py:162
  18.3 0.0 collective-permute-done.9.refs_11_
  18.4 1.5 %collective-permute-start.4 = (f32[104,256]{1,0:T(8,128)}, f32[104,256]{1,0:T(8,128)S(1)}, u32[]{:S(2)}, u32[]{:S(2)}) collective-permute-start(f32[104,256]{1,0:T(8,128)} %centre_pack.1.refs_4_), channel_id=1, source_target_pairs={{0,8},{4,12},{8,16},{12,20},{16,24},{20,28},{24,0},{28,4},{1,9},{5... | collective-permute-start | bytes 319496 | tf_op jit(solution)/shard_map/ppermute | solution.py:162
  19.8 0.0 collective-permute-done.8.refs_10_
  19.8 0.0 collective-permute-start.3
  19.8 0.9 %collective-permute-done.7.refs_9_ = f32[104,256]{1,0:T(8,128)S(1)} collective-permute-done((f32[104,256]{1,0:T(8,128)}, f32[104,256]{1,0:T(8,128)S(1)}, u32[]{:S(2)}, u32[]{:S(2)}) %collective-permute-start.7) | collective-permute-done | bytes 106528 | tf_op jit(solution)/shard_map/ppermute | solution.py:162
  20.7 6.3 %collective-permute-done.6.refs_8_ = f32[104,256]{1,0:T(8,128)S(1)} collective-permute-done((f32[104,256]{1,0:T(8,128)}, f32[104,256]{1,0:T(8,128)S(1)}, u32[]{:S(2)}, u32[]{:S(2)}) %collective-permute-start.6) | collective-permute-done | bytes 106528 | tf_op jit(solution)/shard_map/ppermute | solution.py:162
  27.0 0.8 %collective-permute-done.5.refs_7_ = f32[104,256]{1,0:T(8,128)S(1)} collective-permute-done((f32[104,256]{1,0:T(8,128)}, f32[104,256]{1,0:T(8,128)S(1)}, u32[]{:S(2)}, u32[]{:S(2)}) %collective-permute-start.5) | collective-permute-done | bytes 106528 | tf_op jit(solution)/shard_map/ppermute | solution.py:162
  27.8 0.0 collective-permute-done.4.refs_6_
  27.8 0.0 collective-permute-done.3.refs_5_
  27.8 0.9 %copy-done = f32[104,256]{1,0:T(8,128)S(1)} copy-done((f32[104,256]{1,0:T(8,128)S(1)}, f32[104,256]{1,0:T(8,128)}, u32[]{:S(2)}) %copy-start) | copy-done | bytes 106520
  28.7 2.2 %kernel_tile.1 = (f32[32,128]{1,0:T(8,128)S(1)}, f32[32,128]{1,0:T(8,128)S(1)}, f32[32,128]{1,0:T(8,128)S(1)}, f32[32,128]{1,0:T(8,128)S(1)}) custom-call(f32[3,32,256]{2,1,0:T(8,128)S(1)} %copy-done.1, f32[3,32,256]{2,1,0:T(8,128)S(1)} %collective-permute-done.refs_1_, f32[3,32,256]{2,1,0:T(8,128)S(1)} %collective-permute-done.1.refs_2_, ...), custom_call_target="tpu_custom_call" | custom-call | tf_op jit(solution)/shard_map/kernel_tile/pallas_call | solution.py:166
  30.9 0.6 %copy-done.2 = f32[32,128]{1,0:T(8,128)} copy-done((f32[32,128]{1,0:T(8,128)}, f32[32,128]{1,0:T(8,128)S(1)}, u32[]{:S(2)}) %copy-start.2) | copy-done | bytes 16408
  31.5 2.4 %collective-permute-start.10 = (f32[32,128]{1,0:T(8,128)S(1)}, f32[32,128]{1,0:T(8,128)S(1)}, u32[]{:S(2)}, u32[]{:S(2)}) collective-permute-start(f32[32,128]{1,0:T(8,128)S(1)} %get-tuple-element.10), channel_id=1, source_target_pairs={{0,3},{1,0},{2,1},{3,2},{4,7},{5,4},{6,5},{7,6},{8,11},{9,8},{10,9... | collective-permute-start | bytes 49160 | tf_op jit(solution)/shard_map/ppermute | solution.py:179
  33.9 1.0 %collective-permute-start.11 = (f32[32,128]{1,0:T(8,128)S(1)}, f32[32,128]{1,0:T(8,128)S(1)}, u32[]{:S(2)}, u32[]{:S(2)}) collective-permute-start(f32[32,128]{1,0:T(8,128)S(1)} %get-tuple-element.11), channel_id=1, source_target_pairs={{0,2},{1,3},{2,0},{3,1},{4,6},{5,7},{6,4},{7,5},{8,10},{9,11},{10,... | collective-permute-start | bytes 49160 | tf_op jit(solution)/shard_map/ppermute | solution.py:179
  34.9 2.0 %collective-permute-start.12 = (f32[32,128]{1,0:T(8,128)S(1)}, f32[32,128]{1,0:T(8,128)S(1)}, u32[]{:S(2)}, u32[]{:S(2)}) collective-permute-start(f32[32,128]{1,0:T(8,128)S(1)} %get-tuple-element.12), channel_id=1, source_target_pairs={{0,1},{1,2},{2,3},{3,0},{4,5},{5,6},{6,7},{7,4},{8,9},{9,10},{10,1... | collective-permute-start | bytes 49160 | tf_op jit(solution)/shard_map/ppermute | solution.py:179
  36.9 0.0 collective-permute-done.10.refs_1_
  36.9 1.6 %collective-permute-done.11.refs_2_ = f32[32,128]{1,0:T(8,128)S(1)} collective-permute-done((f32[32,128]{1,0:T(8,128)S(1)}, f32[32,128]{1,0:T(8,128)S(1)}, u32[]{:S(2)}, u32[]{:S(2)}) %collective-permute-start.11) | collective-permute-done | bytes 16416 | tf_op jit(solution)/shard_map/ppermute | solution.py:179
  38.5 1.9 %collective-permute-done.12.refs_3_ = f32[32,128]{1,0:T(8,128)S(1)} collective-permute-done((f32[32,128]{1,0:T(8,128)S(1)}, f32[32,128]{1,0:T(8,128)S(1)}, u32[]{:S(2)}, u32[]{:S(2)}) %collective-permute-start.12) | collective-permute-done | bytes 16416 | tf_op jit(solution)/shard_map/ppermute | solution.py:179
  40.4 0.6 %copy-done.5 = f32[32,128]{1,0:T(8,128)} copy-done((f32[32,128]{1,0:T(8,128)}, f32[32,128]{1,0:T(8,128)S(1)}, u32[]{:S(2)}) %copy-start.5) | copy-done | bytes 16408
  41.0 1.5 %sum_divide.1 = f32[32,64]{1,0:T(8,128)} custom-call(f32[32,128]{1,0:T(8,128)} %copy-done.2, f32[32,128]{1,0:T(8,128)} %copy-done.3, f32[32,128]{1,0:T(8,128)} %copy-done.4, f32[32,128]{1,0:T(8,128)} %copy-done.5), custom_call_target="tpu_custom_call" | custom-call | tf_op jit(solution)/shard_map/sum_divide/pallas_call | solution.py:182
  (9 shorter events, 0.0 us)
Async XLA Ops:
  0.0 5.6 %copy-start.1 = (f32[3,32,256]{2,1,0:T(8,128)S(1)}, f32[3,32,256]{2,1,0:T(8,128)}, u32[]{:S(2)}) copy-start(f32[3,32,256]{2,1,0:T(8,128)} %refs_0_.1) | copy-start | bytes 294916
  1.7 16.7 %collective-permute-start.9 = (f32[104,256]{1,0:T(8,128)}, f32[104,256]{1,0:T(8,128)S(1)}, u32[]{:S(2)}, u32[]{:S(2)}) collective-permute-start(f32[104,256]{1,0:T(8,128)} %centre_pack.1.refs_4_), channel_id=1, source_target_pairs={{0,28},{4,0},{8,4},{12,8},{16,12},{20,16},{24,20},{28,24},{1,29},{... | collective-permute-start | bytes 319496 | tf_op jit(solution)/shard_map/ppermute | solution.py:162
  5.0 14.8 %collective-permute-start.8 = (f32[104,256]{1,0:T(8,128)}, f32[104,256]{1,0:T(8,128)S(1)}, u32[]{:S(2)}, u32[]{:S(2)}) collective-permute-start(f32[104,256]{1,0:T(8,128)} %centre_pack.1.refs_4_), channel_id=1, source_target_pairs={{0,24},{4,28},{8,0},{12,4},{16,8},{20,12},{24,16},{28,20},{1,25},{... | collective-permute-start | bytes 319496 | tf_op jit(solution)/shard_map/ppermute | solution.py:162
  5.6 10.8 %collective-permute-start.1 = (f32[3,32,256]{2,1,0:T(8,128)S(1)}, f32[3,32,256]{2,1,0:T(8,128)S(1)}, u32[]{:S(2)}, u32[]{:S(2)}) collective-permute-start(f32[3,32,256]{2,1,0:T(8,128)S(1)} %copy-done.1), channel_id=1, source_target_pairs={{0,2},{1,3},{2,0},{3,1},{4,6},{5,7},{6,4},{7,5},{8,10},{9,11},{10,... | collective-permute-start | bytes 294920 | tf_op jit(solution)/shard_map/ppermute | solution.py:151
  8.2 8.2 %collective-permute-start = (f32[3,32,256]{2,1,0:T(8,128)S(1)}, f32[3,32,256]{2,1,0:T(8,128)S(1)}, u32[]{:S(2)}, u32[]{:S(2)}) collective-permute-start(f32[3,32,256]{2,1,0:T(8,128)S(1)} %copy-done.1), channel_id=1, source_target_pairs={{0,1},{1,2},{2,3},{3,0},{4,5},{5,6},{6,7},{7,4},{8,9},{9,10},{10,1... | collective-permute-start | bytes 294920 | tf_op jit(solution)/shard_map/ppermute | solution.py:151
  9.7 7.5 %collective-permute-start.2 = (f32[3,32,256]{2,1,0:T(8,128)S(1)}, f32[3,32,256]{2,1,0:T(8,128)S(1)}, u32[]{:S(2)}, u32[]{:S(2)}) collective-permute-start(f32[3,32,256]{2,1,0:T(8,128)S(1)} %copy-done.1), channel_id=1, source_target_pairs={{0,3},{1,0},{2,1},{3,2},{4,7},{5,4},{6,5},{7,6},{8,11},{9,8},{10,9... | collective-permute-start | bytes 294920 | tf_op jit(solution)/shard_map/ppermute | solution.py:151
  16.4 4.3 %collective-permute-start.7 = (f32[104,256]{1,0:T(8,128)}, f32[104,256]{1,0:T(8,128)S(1)}, u32[]{:S(2)}, u32[]{:S(2)}) collective-permute-start(f32[104,256]{1,0:T(8,128)} %centre_pack.1.refs_4_), channel_id=1, source_target_pairs={{0,20},{4,24},{8,28},{12,0},{16,4},{20,8},{24,12},{28,16},{1,21},{... | collective-permute-start | bytes 319496 | tf_op jit(solution)/shard_map/ppermute | solution.py:162
  16.4 10.6 %collective-permute-start.6 = (f32[104,256]{1,0:T(8,128)}, f32[104,256]{1,0:T(8,128)S(1)}, u32[]{:S(2)}, u32[]{:S(2)}) collective-permute-start(f32[104,256]{1,0:T(8,128)} %centre_pack.1.refs_4_), channel_id=1, source_target_pairs={{0,16},{4,20},{8,24},{12,28},{16,0},{20,4},{24,8},{28,12},{1,17},{... | collective-permute-start | bytes 319496 | tf_op jit(solution)/shard_map/ppermute | solution.py:162
  17.2 10.6 %collective-permute-start.5 = (f32[104,256]{1,0:T(8,128)}, f32[104,256]{1,0:T(8,128)S(1)}, u32[]{:S(2)}, u32[]{:S(2)}) collective-permute-start(f32[104,256]{1,0:T(8,128)} %centre_pack.1.refs_4_), channel_id=1, source_target_pairs={{0,12},{4,16},{8,20},{12,24},{16,28},{20,0},{24,4},{28,8},{1,13},{... | collective-permute-start | bytes 319496 | tf_op jit(solution)/shard_map/ppermute | solution.py:162
  18.4 9.4 %collective-permute-start.4 = (f32[104,256]{1,0:T(8,128)}, f32[104,256]{1,0:T(8,128)S(1)}, u32[]{:S(2)}, u32[]{:S(2)}) collective-permute-start(f32[104,256]{1,0:T(8,128)} %centre_pack.1.refs_4_), channel_id=1, source_target_pairs={{0,8},{4,12},{8,16},{12,20},{16,24},{20,28},{24,0},{28,4},{1,9},{5... | collective-permute-start | bytes 319496 | tf_op jit(solution)/shard_map/ppermute | solution.py:162
  19.8 8.0 %collective-permute-start.3 = (f32[104,256]{1,0:T(8,128)}, f32[104,256]{1,0:T(8,128)S(1)}, u32[]{:S(2)}, u32[]{:S(2)}) collective-permute-start(f32[104,256]{1,0:T(8,128)} %centre_pack.1.refs_4_), channel_id=1, source_target_pairs={{0,4},{4,8},{8,12},{12,16},{16,20},{20,24},{24,28},{28,0},{1,5},{5... | collective-permute-start | bytes 319496 | tf_op jit(solution)/shard_map/ppermute | solution.py:162
  27.8 0.9 %copy-start = (f32[104,256]{1,0:T(8,128)S(1)}, f32[104,256]{1,0:T(8,128)}, u32[]{:S(2)}) copy-start(f32[104,256]{1,0:T(8,128)} %centre_pack.1.refs_4_) | copy-start | bytes 319492
  30.9 0.6 %copy-start.2 = (f32[32,128]{1,0:T(8,128)}, f32[32,128]{1,0:T(8,128)S(1)}, u32[]{:S(2)}) copy-start(f32[32,128]{1,0:T(8,128)S(1)} %get-tuple-element.9.refs_0_) | copy-start | bytes 49156
  31.5 5.4 %collective-permute-start.10 = (f32[32,128]{1,0:T(8,128)S(1)}, f32[32,128]{1,0:T(8,128)S(1)}, u32[]{:S(2)}, u32[]{:S(2)}) collective-permute-start(f32[32,128]{1,0:T(8,128)S(1)} %get-tuple-element.10), channel_id=1, source_target_pairs={{0,3},{1,0},{2,1},{3,2},{4,7},{5,4},{6,5},{7,6},{8,11},{9,8},{10,9... | collective-permute-start | bytes 49160 | tf_op jit(solution)/shard_map/ppermute | solution.py:179
  33.9 4.6 %collective-permute-start.11 = (f32[32,128]{1,0:T(8,128)S(1)}, f32[32,128]{1,0:T(8,128)S(1)}, u32[]{:S(2)}, u32[]{:S(2)}) collective-permute-start(f32[32,128]{1,0:T(8,128)S(1)} %get-tuple-element.11), channel_id=1, source_target_pairs={{0,2},{1,3},{2,0},{3,1},{4,6},{5,7},{6,4},{7,5},{8,10},{9,11},{10,... | collective-permute-start | bytes 49160 | tf_op jit(solution)/shard_map/ppermute | solution.py:179
  34.9 5.5 %collective-permute-start.12 = (f32[32,128]{1,0:T(8,128)S(1)}, f32[32,128]{1,0:T(8,128)S(1)}, u32[]{:S(2)}, u32[]{:S(2)}) collective-permute-start(f32[32,128]{1,0:T(8,128)S(1)} %get-tuple-element.12), channel_id=1, source_target_pairs={{0,1},{1,2},{2,3},{3,0},{4,5},{5,6},{6,7},{7,4},{8,9},{9,10},{10,1... | collective-permute-start | bytes 49160 | tf_op jit(solution)/shard_map/ppermute | solution.py:179
  36.9 3.5 %copy-start.3 = (f32[32,128]{1,0:T(8,128)}, f32[32,128]{1,0:T(8,128)S(1)}, u32[]{:S(2)}) copy-start(f32[32,128]{1,0:T(8,128)S(1)} %collective-permute-done.10.refs_1_) | copy-start | bytes 49156
  38.5 1.9 %copy-start.4 = (f32[32,128]{1,0:T(8,128)}, f32[32,128]{1,0:T(8,128)S(1)}, u32[]{:S(2)}) copy-start(f32[32,128]{1,0:T(8,128)S(1)} %collective-permute-done.11.refs_2_) | copy-start | bytes 49156
  40.4 0.6 %copy-start.5 = (f32[32,128]{1,0:T(8,128)}, f32[32,128]{1,0:T(8,128)S(1)}, u32[]{:S(2)}) copy-start(f32[32,128]{1,0:T(8,128)S(1)} %collective-permute-done.12.refs_3_) | copy-start | bytes 49156
